TPU v7x, 256 devices: a whole 4x4x8 slice. The times are simulated.
256 devices in a mesh: dp: 8 (over y, core), rows: 32 (over x, z).
Axes of the slice: x: 4, y: 4, z: 8, core: 2. Of those that a mesh axis runs over, the one named last changes fastest.
Arguments:
- image_tokens: bfloat16 [8, 256, 32, 512], P('dp', 'rows'), may hold values from -6 to 6
- top_cond: float32 [8, 512], P('dp'), may hold values from 0.5 to 2
- bottom_cond: float32 [8, 1024], P('dp'), may hold values from 0.5 to 2
- top_qkv: bfloat16 [512, 1536], P('rows'), may hold values from -0.25 to 0.25
- top_scale: float32 [8], replicated, may hold values from 4 to 16
- merge_weight: bfloat16 [2048, 1024], P('rows'), may hold values from -0.125 to 0.125
- bottom_qkv: bfloat16 [1024, 3072], P('rows'), may hold values from -0.1875 to 0.1875
- bottom_scale: float32 [16], replicated, may hold values from 4 to 16
- out_cotangent: bfloat16 [8, 128, 16, 1024], P('dp', 'rows'), may hold values from -6 to 6
Outputs:
- output: bfloat16 [8, 128, 16, 1024], P('dp', 'rows')
- grad_tokens: bfloat16 [8, 256, 32, 512], P('dp', 'rows')
- top_qkv_grad: float32 [512, 1536], P('rows', 'dp')
- merge_grad: float32 [2048, 1024], P('rows', 'dp')
- low_qkv_grad: float32 [1024, 3072], P('rows', 'dp')
All inputs are finite; a program needn't handle non-finite values.
Results may differ from a plain program's by a relative error of at most 0.035.
Values may be sent and summed in bfloat16 or wider, within the bound.
No kernel may reach another device: no remote copies, remote signals or barrier semaphores. Data moves between devices by JAX's collectives and lax.ppermute only.
A program may use at most 192 MiB of HBM per device.

v0:
```python
import jax
import jax.numpy as jnp
from jax import lax
from jax.sharding import PartitionSpec as P

epsilon = 1e-06


def with_halo(block, sides, width):
    for axis, dim in sides:
        count = lax.axis_size(axis)
        forward = [(i, i + 1) for i in range(count - 1)]
        backward = [(target, source) for source, target in forward]
        low = lax.ppermute(
            lax.slice_in_dim(block, block.shape[dim] - width, None, axis=dim), axis, forward
        )
        high = lax.ppermute(lax.slice_in_dim(block, 0, width, axis=dim), axis, backward)
        block = jnp.concatenate([low, block, high], axis=dim)
    return block


def from_behind(block, axis, distance):
    devices = range(lax.axis_size(axis))
    route = [(i - distance, i) for i in devices if i - distance in devices]
    return lax.ppermute(block, axis, route)


def rms_scale(values, gains):
    mean_sq = jnp.mean(values * values, axis=-1, keepdims=True)
    return values * lax.rsqrt(mean_sq + epsilon) * gains


def head_norm(values, head_count):
    shaped = values.reshape(values.shape[:-1] + (head_count, values.shape[-1] // head_count))
    mean_sq = jnp.mean(shaped * shaped, axis=-1, keepdims=True)
    return shaped * lax.rsqrt(mean_sq + epsilon)


def neighbour_attend(queries, keys, values, scales, first_row, grid_rows):
    query_rows, grid_cols, features = queries.shape
    head_count = scales.shape[0]
    head_size = features // head_count
    query_unit = head_norm(queries, head_count)
    key_unit = jnp.pad(head_norm(keys, head_count), ((0, 0), (3, 3), (0, 0), (0, 0)))
    value_heads = jnp.pad(
        values.reshape(keys.shape[0], grid_cols, head_count, head_size),
        ((0, 0), (3, 3), (0, 0), (0, 0)),
    )
    row_pos = first_row + jnp.arange(query_rows, dtype=jnp.int32)
    col_pos = jnp.arange(grid_cols, dtype=jnp.int32)

    def one_row(carry, row_shift):
        numer, denom = carry
        key_rows = lax.dynamic_slice_in_dim(key_unit, row_shift, query_rows, 0)
        value_rows = lax.dynamic_slice_in_dim(value_heads, row_shift, query_rows, 0)
        key_row = row_pos + row_shift - 3
        row_ok = (key_row >= 0) & (key_row < grid_rows)
        for col_shift in range(7):
            key_part = key_rows[:, col_shift : col_shift + grid_cols]
            value_part = value_rows[:, col_shift : col_shift + grid_cols]
            key_col = col_pos + col_shift - 3
            col_ok = (key_col >= 0) & (key_col < grid_cols)
            inside = (row_ok[:, None] & col_ok[None, :]).astype(jnp.float32)
            score = scales * jnp.mean(query_unit * key_part, axis=-1)
            weight = jnp.exp(score) * inside[:, :, None]
            numer = numer + weight[..., None] * value_part
            denom = denom + weight
        return ((numer, denom), None)

    start = (
        jnp.zeros(query_unit.shape, jnp.float32),
        jnp.zeros(query_unit.shape[:-1], jnp.float32),
    )
    (numer, denom), _ = lax.scan(jax.checkpoint(one_row), start, jnp.arange(7, dtype=jnp.int32))
    return (numer / denom[..., None]).reshape(query_rows, grid_cols, features)


def global_attend(queries, keys, values, scales):
    depth = queries.shape[-1]
    query_unit = queries * lax.rsqrt(jnp.mean(queries * queries, axis=-1, keepdims=True) + epsilon)
    key_unit = keys * lax.rsqrt(jnp.mean(keys * keys, axis=-1, keepdims=True) + epsilon)
    score = jnp.einsum("qhd,khd->hqk", query_unit, key_unit) * (scales[:, None, None] / depth)
    weight = jnp.exp(score)
    probs = weight / jnp.sum(weight, axis=-1, keepdims=True)
    return jnp.einsum("hqk,khd->qhd", probs, values)


def unshuffle(grid):
    grid_rows, grid_cols, features = grid.shape
    split = grid.reshape(grid_rows // 2, 2, grid_cols // 2, 2, features).transpose(0, 2, 1, 3, 4)
    return split.reshape(grid_rows // 2 * (grid_cols // 2), 4 * features)


def shuffle(flat, grid_rows, grid_cols, features):
    split = flat.reshape(grid_rows // 2, grid_cols // 2, 2, 2, features).transpose(0, 2, 1, 3, 4)
    return split.reshape(grid_rows, grid_cols, features)


def contract_rows(left, right):
    return lax.dot_general(
        left, right, (((0,), (0,)), ((), ())), preferred_element_type=jnp.float32
    )


def contract_cols(left, right):
    return lax.dot_general(
        left, right, (((1,), (1,)), ((), ())), preferred_element_type=jnp.float32
    )


def body(
    image_tokens,
    top_cond,
    bottom_cond,
    top_qkv,
    top_scale,
    merge_weight,
    bottom_qkv,
    bottom_scale,
    out_cotangent,
):
    shard_rows, grid_cols, top_width = image_tokens.shape[1:]
    low_width = bottom_cond.shape[1]
    head_count = bottom_scale.shape[0]
    head_size = low_width // head_count
    row_devices = lax.axis_size("rows")
    grid_rows = shard_rows * row_devices
    first_row = lax.axis_index("rows") * shard_rows
    w_top, w_merge, w_low = (
        lax.all_gather(top_qkv, "rows", axis=0, tiled=True),
        lax.all_gather(merge_weight, "rows", axis=0, tiled=True),
        lax.all_gather(bottom_qkv, "rows", axis=0, tiled=True),
    )
    tokens_f = image_tokens[0].astype(jnp.float32)
    top_normed = rms_scale(tokens_f, top_cond[0]).astype(jnp.bfloat16)
    top_flat = top_normed.reshape(shard_rows * grid_cols, top_width)
    top_proj = jnp.dot(top_flat, w_top, preferred_element_type=jnp.float32).astype(jnp.bfloat16)
    top_proj = top_proj.reshape(shard_rows, grid_cols, 3 * top_width)
    query_top = top_proj[..., :top_width]
    key_value = jnp.stack(
        [top_proj[..., top_width : 2 * top_width], top_proj[..., 2 * top_width :]]
    )

    def local_top(query_part, key_part, value_part, start_row):
        return neighbour_attend(query_part, key_part, value_part, top_scale, start_row, grid_rows)

    key_ext = with_halo(key_value, (("rows", 1),), 3)
    top_out, top_pull = jax.vjp(
        lambda query_part, key_part, value_part: local_top(
            query_part, key_part, value_part, first_row
        ),
        query_top.astype(jnp.float32),
        key_ext[0].astype(jnp.float32),
        key_ext[1].astype(jnp.float32),
    )
    middle = (tokens_f + top_out).astype(jnp.bfloat16)
    unshuffled = unshuffle(middle)
    low = jnp.dot(unshuffled, w_merge, preferred_element_type=jnp.float32).astype(jnp.bfloat16)
    low_f = low.astype(jnp.float32)
    low_normed = rms_scale(low_f, bottom_cond[0]).astype(jnp.bfloat16)
    low_proj = jnp.dot(low_normed, w_low, preferred_element_type=jnp.float32).astype(jnp.bfloat16)
    low_count = low.shape[0]
    heads_here = max(head_count // row_devices, 1)
    head_groups = head_count // heads_here
    query_shares = row_devices // head_groups
    group_width = heads_here * head_size
    share_rows = low_count // query_shares
    cotangent = out_cotangent[0].reshape(low_count, low_width)

    def grouped(block):
        return block.reshape(low_count, head_groups, group_width)

    query_side = jnp.concatenate([grouped(low_proj[:, :low_width]), grouped(cotangent)], axis=-1)
    query_side = query_side.reshape(
        query_shares, share_rows, head_groups, 2 * group_width
    ).transpose(2, 0, 1, 3)
    query_side = query_side.reshape(row_devices, share_rows, 2 * group_width)
    key_side = jnp.concatenate(
        [grouped(low_proj[:, low_width : 2 * low_width]), grouped(low_proj[:, 2 * low_width :])],
        axis=-1,
    )
    key_side = jnp.repeat(key_side.transpose(1, 0, 2), query_shares, axis=0)
    query_in, key_in = (
        lax.all_to_all(query_side, "rows", split_axis=0, concat_axis=1, tiled=True),
        lax.all_to_all(key_side, "rows", split_axis=0, concat_axis=1, tiled=True),
    )
    query_all = query_in[0]
    key_all = key_in[0]
    seq_queries = query_all.shape[0]
    seq_keys = key_all.shape[0]
    queries = query_all[:, :group_width].reshape(seq_queries, heads_here, head_size)
    grads_in = (
        query_all[:, group_width:].astype(jnp.float32).reshape(seq_queries, heads_here, head_size)
    )
    keys = key_all[:, :group_width].astype(jnp.float32).reshape(seq_keys, heads_here, head_size)
    values = key_all[:, group_width:].astype(jnp.float32).reshape(seq_keys, heads_here, head_size)
    group_index = lax.axis_index("rows") // query_shares
    scales_here = lax.dynamic_slice_in_dim(bottom_scale, group_index * heads_here, heads_here)
    block_rows = min(512, seq_queries)
    block_count = seq_queries // block_rows

    def one_block(carry, items):
        query_block, grad_block = items

        def attend_low(query_part, key_part, value_part):
            return global_attend(query_part, key_part, value_part, scales_here)

        attended, pull = jax.vjp(attend_low, query_block.astype(jnp.float32), keys, values)
        grad_q, grad_k, grad_v = pull(grad_block)
        return (
            (carry[0] + grad_k, carry[1] + grad_v),
            (attended.astype(jnp.bfloat16), grad_q.astype(jnp.bfloat16)),
        )

    zero_grads = jnp.zeros_like(keys)
    block_items = (
        queries.reshape(block_count, block_rows, heads_here, head_size),
        grads_in.reshape(block_count, block_rows, heads_here, head_size),
    )
    (key_grads, value_grads), (out_blocks, query_grads) = lax.scan(
        one_block, (zero_grads, zero_grads), block_items
    )
    back_query = jnp.concatenate(
        [
            out_blocks.reshape(seq_queries, group_width),
            query_grads.reshape(seq_queries, group_width),
        ],
        axis=-1,
    )
    back_query = back_query.reshape(row_devices, share_rows, 2 * group_width)
    back_key = jnp.concatenate(
        [key_grads.reshape(seq_keys, group_width), value_grads.reshape(seq_keys, group_width)],
        axis=-1,
    )
    back_key = back_key.reshape(row_devices, low_count, 2 * group_width)
    ret_query = lax.all_to_all(back_query, "rows", split_axis=0, concat_axis=0, tiled=True)
    ret_key = lax.all_to_all(
        back_key.astype(jnp.bfloat16), "rows", split_axis=0, concat_axis=0, tiled=True
    ).astype(back_key.dtype)
    ret_query = ret_query.reshape(head_groups, query_shares, share_rows, 2 * group_width).transpose(
        1, 2, 0, 3
    )
    ret_query = ret_query.reshape(low_count, head_groups, 2 * group_width)
    ret_key = jnp.sum(
        ret_key.reshape(head_groups, query_shares, low_count, 2 * group_width), axis=1
    ).transpose(1, 0, 2)
    low_attention = ret_query[..., :group_width].reshape(low_count, low_width)
    grad_query_low = ret_query[..., group_width:].reshape(low_count, low_width)
    grad_key_low = ret_key[..., :group_width].reshape(low_count, low_width).astype(jnp.bfloat16)
    grad_value_low = ret_key[..., group_width:].reshape(low_count, low_width).astype(jnp.bfloat16)
    output = (low_f + low_attention.astype(jnp.float32)).astype(jnp.bfloat16)
    grad_low_proj = jnp.concatenate([grad_query_low, grad_key_low, grad_value_low], axis=-1)
    back_low = contract_cols(grad_low_proj, w_low)
    _, pull_low = jax.vjp(lambda low_in: rms_scale(low_in, bottom_cond[0]), low_f)
    grad_low = (cotangent.astype(jnp.float32) + pull_low(back_low)[0]).astype(jnp.bfloat16)
    grad_middle = shuffle(contract_cols(grad_low, w_merge), shard_rows, grid_cols, top_width)
    grad_q1, grad_k_ext, grad_v_ext = top_pull(grad_middle)
    upper = jnp.stack([grad_k_ext[:3], grad_v_ext[:3]])
    lower = jnp.stack([grad_k_ext[-3:], grad_v_ext[-3:]])
    from_next = from_behind(upper.astype(jnp.bfloat16), "rows", -1).astype(upper.dtype)
    from_prev = from_behind(lower.astype(jnp.bfloat16), "rows", 1).astype(lower.dtype)
    grad_k1 = grad_k_ext[3:-3].at[:3].add(from_prev[0]).at[-3:].add(from_next[0])
    grad_v1 = grad_v_ext[3:-3].at[:3].add(from_prev[1]).at[-3:].add(from_next[1])
    grad_top_proj = jnp.concatenate([grad_q1, grad_k1, grad_v1], axis=-1).astype(jnp.bfloat16)
    grad_top_flat = grad_top_proj.reshape(shard_rows * grid_cols, 3 * top_width)
    back_top = contract_cols(grad_top_flat, w_top).reshape(shard_rows, grid_cols, top_width)
    _, pull_top = jax.vjp(lambda top_in: rms_scale(top_in, top_cond[0]), tokens_f)
    grad_tokens = (grad_middle + pull_top(back_top)[0]).astype(jnp.bfloat16)
    part_low = contract_rows(low_normed, grad_low_proj)
    section_low = lax.psum_scatter(
        part_low.astype(jnp.bfloat16), "rows", scatter_dimension=0, tiled=True
    )
    sum_low = lax.psum_scatter(section_low, "dp", scatter_dimension=1, tiled=True).astype(
        jnp.float32
    )
    part_top = contract_rows(top_flat, grad_top_flat)
    part_merge = contract_rows(unshuffled, grad_low)
    section_top, section_merge = (
        lax.psum_scatter(
            part_top.astype(jnp.bfloat16), "rows", scatter_dimension=0, tiled=True
        ).astype(jnp.float32),
        lax.psum_scatter(
            part_merge.astype(jnp.bfloat16), "rows", scatter_dimension=0, tiled=True
        ).astype(jnp.float32),
    )
    sum_top, sum_merge = (
        lax.psum_scatter(
            section_top.astype(jnp.bfloat16), "dp", scatter_dimension=1, tiled=True
        ).astype(jnp.float32),
        lax.psum_scatter(
            section_merge.astype(jnp.bfloat16), "dp", scatter_dimension=1, tiled=True
        ).astype(jnp.float32),
    )
    low_rows = shard_rows // 2
    low_cols = grid_cols // 2
    return (
        output.reshape(1, low_rows, low_cols, low_width),
        grad_tokens[None],
        sum_top,
        sum_merge,
        sum_low,
    )


def solution(mesh):
    placed = (
        P("dp", "rows", None, None),
        P("dp", None),
        P("dp", None),
        P("rows", None),
        P(),
        P("rows", None),
        P("rows", None),
        P(),
        P("dp", "rows", None, None),
    )
    return jax.shard_map(
        body,
        mesh=mesh,
        in_specs=placed,
        out_specs=(
            P("dp", "rows", None, None),
            P("dp", "rows", None, None),
            P("rows", "dp"),
            P("rows", "dp"),
            P("rows", "dp"),
        ),
        check_vma=False,
    )
```

profile of v0, /device:TPU:2, one launch (start us, length us, event | category | flops | bytes accessed | tf_op | source)
XLA Modules:
  0.0 1444.7 jit_solution(9351130730363340344)
XLA Ops:
  15.6 74.0 %all-gather.4.cloned.1.call-done = bf16[512,1536]{1,0:T(8,128)(2,1)} async-done(((bf16[16,1536]{1,0:T(8,128)(2,1)}), bf16[512,1536]{1,0:T(8,128)(2,1)}) %all-gather.4.cloned.1.call-update) | async-done | bytes 1572880 | tf_op jit(solution)/shard_map/all_gather | solution.py:130
  113.9 102.0 %while.63 = (s32[]{:T(128)}, f32[8,32,8,64]{3,2,1,0:T(8,128)}, f32[8,32,8]{2,1,0:T(8,128)}, s32[7]{0:T(128)S(1)}, f32[14,38,8,64]{3,2,1,0:T(8,128)S(1)}, /*index...) while((s32[]{:T(128)}, f32[8,32,8,64]{3,2,1,0:T(8,128)}, ...), condition=%wide.region_11.12_spmd.clone, body=%wide.region_3.11_spmd.clone.sunk | while | flops 3836260 | bytes 9173910 | solution.py:74
  122.0 6.4 fusion.176
  136.6 6.5 fusion.176
  151.2 6.7 fusion.176
  165.9 6.3 fusion.176
  180.3 6.5 fusion.176
  194.8 6.5 fusion.176
  209.5 6.5 fusion.176
  226.7 33.3 %all-gather.8.cloned.1.call-done = bf16[1024,3072]{1,0:T(8,128)(2,1)} async-done(((bf16[32,3072]{1,0:T(8,128)(2,1)}), bf16[1024,3072]{1,0:T(8,128)(2,1)}) %all-gather.8.cloned.1.call-update) | async-done | bytes 6291472 | tf_op jit(solution)/shard_map/all_gather | solution.py:132
  267.9 7.0 all-to-all-start
  287.7 5.8 all-to-all-start.1
  296.9 10.8 all-to-all-done.1
  321.3 35.2 %while.64 = (s32[]{:T(128)}, f32[2048,1,64]{0,2,1:T(8,128)}, f32[2048,1,64]{0,2,1:T(8,128)}, bf16[2,512,1,64]{1,3,2,0:T(8,128)(2,1)}, bf16[2,512,1,64]{1,3,2,0:T...) while((s32[]{:T(128)}, f32[2048,1,64]{0,2,1:T(8,128)}, ...), condition=%wide.region_20.21_spmd.clone, body=%wide.region_14.0_spmd.clone.sunk | while | flops 820004352 | bytes 90502648 | solution.py:220
  361.2 7.1 all-to-all-start.2
  378.4 8.0 all-to-all-start.3
  432.3 11.7 multiply_reduce_fusion.11
  447.0 181.6 %while.65 = (s32[]{:T(128)}, f32[14,38,8,64]{3,2,1,0:T(8,128)}, f32[14,38,8,64]{3,2,1,0:T(8,128)}, f32[8,32,8,64]{3,2,1,0:T(8,128)}, f32[8,32,8,64]{3,2,1,0:T(8,...) while((s32[]{:T(128)}, f32[14,38,8,64]{3,2,1,0:T(8,128)}, ...), condition=%wide.region_39.40_spmd.clone, body=%wide.region_24.39_spmd.clone.sunk | while | flops 9740709 | bytes 57080472 | solution.py:74
  461.0 6.3 broadcast_multiply_fusion.22
  486.6 6.7 broadcast_multiply_fusion.22
  505.1 5.6 broadcast_multiply_fusion.21
  512.6 6.7 broadcast_multiply_fusion.22
  538.6 6.7 broadcast_multiply_fusion.22
  564.6 6.7 broadcast_multiply_fusion.22
  590.5 6.7 broadcast_multiply_fusion.22
  616.5 6.7 broadcast_multiply_fusion.22
  676.0 204.5 %reduce-scatter.13.cloned.1.call-done = bf16[16,1536]{1,0:T(8,128)(2,1)} async-done(((bf16[512,1536]{1,0:T(8,128)(2,1)}), bf16[16,1536]{1,0:T(8,128)(2,1)}) %reduce-scatter.13.cloned.1.call-update) | async-done | bytes 49168 | tf_op jit(solution)/shard_map/reduce_scatter | solution.py:279
  882.7 221.2 %reduce-scatter.15.cloned.1.call-done = bf16[64,1024]{1,0:T(8,128)(2,1)} async-done(((bf16[2048,1024]{1,0:T(8,128)(2,1)}), bf16[64,1024]{1,0:T(8,128)(2,1)}) %reduce-scatter.15.cloned.1.call-update) | async-done | bytes 131088 | tf_op jit(solution)/shard_map/reduce_scatter | solution.py:282
  1107.4 224.0 %reduce-scatter.17.cloned.1.call-done = bf16[32,3072]{1,0:T(8,128)(2,1)} async-done(((bf16[1024,3072]{1,0:T(8,128)(2,1)}), bf16[32,3072]{1,0:T(8,128)(2,1)}) %reduce-scatter.17.cloned.1.call-update) | async-done | bytes 196624 | tf_op jit(solution)/shard_map/reduce_scatter | solution.py:270
  1334.4 32.0 %reduce-scatter.19.cloned.1.call-done = bf16[192,16]{1,0:T(8,128)(2,1)} async-done(((bf16[1536,16]{1,0:T(8,128)(2,1)}), bf16[192,16]{1,0:T(8,128)(2,1)}) %reduce-scatter.19.cloned.1.call-update) | async-done | bytes 6160
  1367.9 32.9 %reduce-scatter.21.cloned.1.call-done = bf16[128,64]{1,0:T(8,128)(2,1)} async-done(((bf16[1024,64]{1,0:T(8,128)(2,1)}), bf16[128,64]{1,0:T(8,128)(2,1)}) %reduce-scatter.21.cloned.1.call-update) | async-done | bytes 16400
  1402.3 34.0 %reduce-scatter.23.cloned.1.call-done = bf16[384,32]{1,0:T(8,128)(2,1)} async-done(((bf16[3072,32]{1,0:T(8,128)(2,1)}), bf16[384,32]{1,0:T(8,128)(2,1)}) %reduce-scatter.23.cloned.1.call-update) | async-done | bytes 24592
  (639 shorter events, 398.9 us)
Async XLA Ops:
  7.2 82.4 %all-gather.4.cloned.1.call-start = ((), (), s32[]{:S(2)}) async-start(), calls=%async_computation.10 | async-start | bytes 1622016 | tf_op jit(solution)/shard_map/all_gather | solution.py:130
  7.9 215.6 %all-gather.6.cloned.1.call-start = ((), (), s32[]{:S(2)}) async-start(), calls=%async_computation.11 | async-start | bytes 4325376 | tf_op jit(solution)/shard_map/all_gather | solution.py:131
  8.6 251.4 %all-gather.8.cloned.1.call-start = ((), (), s32[]{:S(2)}) async-start(), calls=%async_computation.12 | async-start | bytes 6488064 | tf_op jit(solution)/shard_map/all_gather | solution.py:132
  91.7 8.7 copy-start.33
  91.7 9.7 collective-permute-start
  94.8 8.1 collective-permute-start.1
  223.5 36.5 %copy-start.56 = (f32[1,1024]{1,0:T(1,128)S(1)}, f32[1,1024]{1,0:T(1,128)}, u32[]{:S(2)}) copy-start(f32[1,1024]{1,0:T(1,128)} %param.25) | copy-start | bytes 12292
  226.7 37.4 %copy-start.25 = (f32[64,1024]{1,0:T(8,128)}, f32[64,1024]{1,0:T(8,128)S(1)}, u32[]{:S(2)}) copy-start(f32[64,1024]{1,0:T(8,128)S(1)} %get-tuple-element.1176) | copy-start | bytes 786436
  226.7 195.0 %copy-start.65 = (f32[64]{0:T(128)}, f32[64]{0:T(128)S(1)}, u32[]{:S(2)}) copy-start(f32[64]{0:T(128)S(1)} %fusion.123) | copy-start | bytes 772
  267.9 17.9 %all-to-all-start = ((bf16[32,32,128]{2,1,0:T(8,128)(2,1)}), bf16[32,32,128]{2,1,0:T(8,128)(2,1)S(1)}, u32[]{:S(2)}, u32[]{:S(2)}) async-start(bf16[32,32,128]{2,1,0:T(8,128)(2,1)} %bitcast.333), calls=%async_computation | async-start | bytes 524288 | tf_op jit(solution)/shard_map/all_to_all | solution.py:184
  274.9 18.6 %copy-start.68 = (f32[16]{0:T(128)S(1)}, f32[16]{0:T(128)}, u32[]{:S(2)}) copy-start(f32[16]{0:T(128)} %param.30) | copy-start | bytes 196
  287.7 20.1 %all-to-all-start.1 = ((bf16[32,64,128]{2,1,0:T(8,128)(2,1)}), bf16[32,64,128]{2,1,0:T(8,128)(2,1)}, u32[]{:S(2)}, u32[]{:S(2)}) async-start(bf16[32,64,128]{2,1,0:T(8,128)(2,1)} %bitcast.325), calls=%async_computation.1 | async-start | bytes 1048576 | tf_op jit(solution)/shard_map/all_to_all | solution.py:185
  361.2 17.2 %all-to-all-start.2 = ((bf16[32,32,128]{2,1,0:T(8,128)(2,1)}), bf16[32,32,128]{2,1,0:T(8,128)(2,1)}, u32[]{:S(2)}, u32[]{:S(2)}) async-start(bf16[32,32,128]{2,1,0:T(8,128)(2,1)} %pad_maximum_fusion.5), calls=%async_computation.2 | async-start | bytes 524288 | tf_op jit(solution)/shard_map/all_to_all | solution.py:236
  370.5 16.0 %copy-start.24 = (f32[8,32,8]{2,1,0:T(8,128)S(1)}, f32[8,32,8]{2,1,0:T(8,128)}, u32[]{:S(2)}) copy-start(f32[8,32,8]{2,1,0:T(8,128)} %get-tuple-element.756) | copy-start | bytes 24580
  378.4 21.4 %all-to-all-start.3 = ((bf16[32,64,128]{2,1,0:T(8,128)(2,1)}), bf16[32,64,128]{2,1,0:T(8,128)(2,1)}, u32[]{:S(2)}, u32[]{:S(2)}) async-start(bf16[32,64,128]{2,1,0:T(8,128)(2,1)} %pad_maximum_fusion.2), calls=%async_computation.3 | async-start | bytes 1048576 | tf_op jit(solution)/shard_map/all_to_all | solution.py:237
  386.4 494.1 %reduce-scatter.13.cloned.1.call-start = ((), (), s32[]{:S(2)}) async-start(), calls=%async_computation.13 | async-start | bytes 1622016 | tf_op jit(solution)/shard_map/reduce_scatter | solution.py:279
  590.5 6.7 copy-start.7
  638.0 8.4 copy-start.14
  638.0 8.5 copy-start.20
  638.0 8.5 copy-start.43
  641.2 7.5 copy-start.30
  641.9 19.2 %collective-permute-start.2 = (bf16[2,3,32,512]{3,2,1,0:T(8,128)(2,1)}, bf16[2,3,32,512]{3,2,1,0:T(8,128)(2,1)}, u32[]{:S(2)}, u32[]{:S(2)}) collective-permute-start(bf16[2,3,32,512]{3,2,1,0:T(8,128)(2,1)} %pad_maximum_fusion.8), channel_id=1, source_target_pairs={{0,1},{1,2},{2,3},{3,4},{4,5},{5,6},{6,7},{7,8},{8,9},{9,10},{10,1... | collective-permute-start | bytes 589832 | tf_op jit(solution)/shard_map/ppermute | solution.py:25
  651.6 9.0 copy-start.41
  655.7 7.9 collective-permute-start.3
  666.6 437.3 %reduce-scatter.15.cloned.1.call-start = ((), (), s32[]{:S(2)}) async-start(), calls=%async_computation.14 | async-start | bytes 4325376 | tf_op jit(solution)/shard_map/reduce_scatter | solution.py:282
  670.3 661.1 %reduce-scatter.17.cloned.1.call-start = ((), (), s32[]{:S(2)}) async-start(), calls=%async_computation.15 | async-start | bytes 6488064 | tf_op jit(solution)/shard_map/reduce_scatter | solution.py:270
  675.9 206.4 %copy-start.31 = (f32[4,2,16,2,512]{4,3,2,1,0:T(2,128)S(1)}, f32[4,2,16,2,512]{4,3,2,1,0:T(2,128)}, u32[]{:S(2)}) copy-start(f32[4,2,16,2,512]{4,3,2,1,0:T(2,128)} %copy.155) | copy-start | bytes 1572868
  675.9 429.9 %copy-start.39 = (bf16[512,1536]{1,0:T(8,128)(2,1)S(1)}, bf16[512,1536]{1,0:T(8,128)(2,1)}, u32[]{:S(2)}) copy-start(bf16[512,1536]{1,0:T(8,128)(2,1)} %all-gather.4.cloned.1.call-done) | copy-start | bytes 4718596
  675.9 690.5 %reduce-scatter.19.cloned.1.call-start = ((), (), s32[]{:S(2)}) async-start(), calls=%async_computation.16 | async-start | bytes 442368
  882.3 518.5 %reduce-scatter.21.cloned.1.call-start = ((), (), s32[]{:S(2)}) async-start(), calls=%async_computation.17 | async-start | bytes 294912
  1105.7 227.8 %copy-start.62 = (f32[8,32]{1,0:T(8,128)S(1)}, f32[8,32]{1,0:T(8,128)}, u32[]{:S(2)}) copy-start(f32[8,32]{1,0:T(8,128)} %copy-done.61) | copy-start | bytes 3076
  1105.7 330.6 %reduce-scatter.23.cloned.1.call-start = ((), (), s32[]{:S(2)}) async-start(), calls=%async_computation.18 | async-start | bytes 884736
  (120 other events, 487.8 us)
Sparse Core Ops, SparseCore 0:
  10.6 78.9 all-gather.3
  92.2 79.1 all-gather.5
  174.0 86.0 all-gather.7
  666.8 213.7 reduce-scatter.12
  884.3 219.6 reduce-scatter.14
  1108.3 223.0 reduce-scatter.16
  1333.9 32.4 reduce-scatter.18
  1369.0 31.7 reduce-scatter.20
  1403.4 32.9 reduce-scatter.22
where the time goes:
time: 1450 us; the launch traced here: 1440 us
  waiting for transfers between devices  882 us (61%)
  other arithmetic  312 us (22%)
  local copies, waits for them, and re-layouts  113 us (8%)
  matrix products  50.3 us (3%)
  starting transfers between devices  44.4 us (3%)
  loops' own time  26.5 us (2%)
  between operations  15.8 us (1%)
    reduce_scatter x1, waiting for transfers between devices, body(): lax.psum_scatter(part_low.astype(jnp.bfloat16), 'rows', scatter_dimension...  224 us
    reduce_scatter x1, waiting for transfers between devices, body(): lax.psum_scatter(part_merge.astype(jnp.bfloat16), 'rows', scatter_dimensi...  221 us
    reduce_scatter x1, waiting for transfers between devices, body(): lax.psum_scatter(part_top.astype(jnp.bfloat16), 'rows', scatter_dimension...  205 us
    unnamed x12, waiting for transfers between devices  101 us
    all_gather x1, waiting for transfers between devices, body(): lax.all_gather(top_qkv, 'rows', axis=0, tiled=True)  74 us
    mul x21, other arithmetic, one_row(): score = scales * jnp.mean(query_unit * key_part, axis=-1)  46.3 us
    add x7, other arithmetic, one_row(): numer = numer + weight[..., None] * value_part  45.3 us
    mul x7, other arithmetic, one_row(): numer = numer + weight[..., None] * value_part  39.2 us
  transfers between devices with their start and end apart: 17, of which 14 were waited for; matrix products, arithmetic and copies ran while one was open for 12% of the time, Pallas kernels for 0%

commit v1 on v0

v1 whole, which is shorter than its diff:
```python
import functools
import jax
import jax.numpy as jnp
from jax import lax
from jax.experimental import pallas as pl
from jax.experimental.pallas import tpu as pltpu
from jax.sharding import Mesh, PartitionSpec as P

epsilon = 1e-06
log2e = 1.4426950408889634
f32 = jnp.float32
bf16 = jnp.bfloat16
ROWS = ("x", "z")
DP = ("y", "c")
HEAD = 64
MIB = 1 << 20


def dot_nn(left, right):
    return jnp.dot(left, right, preferred_element_type=f32)


def dot_nt(left, right):
    return lax.dot_general(left, right, (((1,), (1,)), ((), ())), preferred_element_type=f32)


def dot_tn(left, right):
    return lax.dot_general(left, right, (((0,), (0,)), ((), ())), preferred_element_type=f32)


def unit_scale(x):
    return lax.rsqrt(jnp.mean(x * x, axis=-1, keepdims=True) + epsilon)


def unit_pull(x, scale, grad):
    inner = jnp.mean(x * grad, axis=-1, keepdims=True)
    return scale * grad - x * (scale * scale * scale * inner)


def grad_ext(grad, out):
    delta = jnp.sum(grad * out, axis=-1, keepdims=True)
    high = delta.astype(bf16).astype(f32)
    rest = delta - high
    lane = lax.broadcasted_iota(jnp.int32, grad.shape, 1)
    tail = jnp.where(lane == 0, -high, jnp.where(lane == 1, -rest, 0.0))
    return jnp.concatenate([grad, tail], axis=1).astype(bf16)


def vmem():
    return pl.BlockSpec(memory_space=pltpu.VMEM)


def smem():
    return pl.BlockSpec(memory_space=pltpu.SMEM)


def anywhere():
    return pl.BlockSpec(memory_space=pl.ANY)


def call(kernel, ins, outs, scratch=(), limit=40, flops=0, name=None):
    return pl.pallas_call(
        kernel,
        in_specs=ins,
        out_specs=[vmem() for _ in outs],
        out_shape=[jax.ShapeDtypeStruct(shape, kind) for shape, kind in outs],
        scratch_shapes=list(scratch),
        compiler_params=pltpu.CompilerParams(vmem_limit_bytes=limit * MIB),
        name=name,
    )


def neighbour_mask(first, grid_rows, cols, query_dim, shape):
    query = lax.broadcasted_iota(jnp.int32, shape, query_dim)
    key = lax.broadcasted_iota(jnp.int32, shape, 1 - query_dim)
    half = cols // 2

    def column(index):
        place = index % cols
        return 2 * (place % half) + place // half

    shift = key // cols - query // cols
    apart = column(key) - column(query)
    key_row = first - 3 + key // cols
    inside = (shift >= 0) & (shift <= 6) & (apart >= -3) & (apart <= 3)
    inside = inside & (key_row >= 0) & (key_row < grid_rows)
    return jnp.where(inside, 1.0, 0.0).astype(f32)


def project_top(pos_ref, flat_ref, own_ref, other_ref, proj_ref, up_ref, down_ref):
    core = pos_ref[1]
    width = own_ref.shape[1]
    tokens, edge = flat_ref.shape[0], up_ref.shape[0]
    here = pl.multiple_of(core * width, 128)
    there = pl.multiple_of((1 - core) * width, 128)
    proj_ref[:, pl.ds(here, width)] = dot_nn(flat_ref[...], own_ref[...]).astype(bf16)
    proj_ref[:, pl.ds(there, width)] = dot_nn(flat_ref[...], other_ref[...]).astype(bf16)
    top = flat_ref.shape[1]
    up_ref[...] = proj_ref[0:edge, top:]
    down_ref[...] = proj_ref[tokens - edge :, top:]


def head_parts(proj_ref, lo_ref, hi_ref, at, top):
    key = jnp.concatenate(
        [
            lo_ref[:, at : at + HEAD],
            proj_ref[:, top + at : top + at + HEAD],
            hi_ref[:, at : at + HEAD],
        ],
        axis=0,
    ).astype(f32)
    value = jnp.concatenate(
        [
            lo_ref[:, top + at : top + at + HEAD],
            proj_ref[:, 2 * top + at : 2 * top + at + HEAD],
            hi_ref[:, top + at : top + at + HEAD],
        ],
        axis=0,
    )
    query = proj_ref[:, at : at + HEAD].astype(f32)
    return query, key, value


def top_forward(
    grid_rows, cols, pos_ref, scale_ref, tok_ref, proj_ref, lo_ref, hi_ref,
    unsh_ref, out_ref, inv_ref, mask_ref,
):
    top = tok_ref.shape[1]
    mask_ref[...] = neighbour_mask(pos_ref[0], grid_rows, cols, 0, mask_ref.shape)
    for pair in range(top // (2 * HEAD)):
        outs, invs = [], []
        for head in (2 * pair, 2 * pair + 1):
            query, key, value = head_parts(proj_ref, lo_ref, hi_ref, head * HEAD, top)
            gain = scale_ref[head] * (log2e / HEAD)
            query = (query * (unit_scale(query) * gain)).astype(bf16)
            key = (key * unit_scale(key)).astype(bf16)
            wide = jnp.concatenate([value, jnp.ones_like(value)], axis=1)
            weight = (jnp.exp2(dot_nt(query, key)) * mask_ref[...]).astype(bf16)
            both = dot_nn(weight, wide)
            inverse = 1.0 / both[:, HEAD:]
            outs.append(both[:, :HEAD] * inverse)
            invs.append(inverse)
        at = pair * 2 * HEAD
        out_ref[:, at : at + 2 * HEAD] = jnp.concatenate(outs, axis=1)
        inv_ref[:, at : at + 2 * HEAD] = jnp.concatenate(invs, axis=1)
    half = cols // 2
    for row in range(tok_ref.shape[0] // cols):
        for odd in range(2):
            at = row * cols + odd * half
            part = tok_ref[at : at + half, :].astype(f32) + out_ref[at : at + half, :]
            low_at = (row // 2) * half
            place = (2 * (row % 2) + odd) * top
            unsh_ref[low_at : low_at + half, place : place + top] = part.astype(bf16)


def top_backward(
    grid_rows, cols, pos_ref, scale_ref, proj_ref, lo_ref, hi_ref, out_ref, inv_ref, grad_ref,
    gq_ref, gmid_ref, gup_ref, gdown_ref, mask_ref,
):
    tokens, top = out_ref.shape
    edge = lo_ref.shape[0]
    mask_ref[...] = neighbour_mask(pos_ref[0], grid_rows, cols, 1, mask_ref.shape)
    for pair in range(top // (2 * HEAD)):
        gqs, gks, gvs = [], [], []
        for head in (2 * pair, 2 * pair + 1):
            at = head * HEAD
            query, key, value = head_parts(proj_ref, lo_ref, hi_ref, at, top)
            gain = scale_ref[head] * (1.0 / HEAD)
            query_scale = unit_scale(query)
            key_scale = unit_scale(key)
            query_unit = (query * (query_scale * (gain * log2e))).astype(bf16)
            key_f = key * key_scale
            key_unit = key_f.astype(bf16)
            key_t = jnp.concatenate([key_f, jnp.zeros_like(key_f)], axis=1).T.astype(bf16)
            wide = jnp.concatenate([value, jnp.ones_like(value)], axis=1)
            grad = grad_ref[:, at : at + HEAD] * inv_ref[:, at : at + HEAD]
            grad = grad_ext(grad, out_ref[:, at : at + HEAD])
            weight = jnp.exp2(dot_nt(key_unit, query_unit)) * mask_ref[...]
            slope = (weight * dot_nt(wide, grad)).astype(bf16)
            gvs.append(dot_nn(weight.astype(bf16), grad)[:, :HEAD])
            gk = dot_nn(slope, query_unit) * (1.0 / log2e)
            gks.append(unit_pull(key, key_scale, gk))
            gq = dot_nn(key_t, slope).T[:, :HEAD] * gain
            gqs.append(unit_pull(query, query_scale, gq))
        at = pair * 2 * HEAD
        gq_ref[:, at : at + 2 * HEAD] = jnp.concatenate(gqs, axis=1).astype(bf16)
        for base, parts in ((at, gks), (top + at, gvs)):
            whole = jnp.concatenate(parts, axis=1)
            gup_ref[:, base : base + 2 * HEAD] = whole[:edge].astype(bf16)
            gmid_ref[:, base : base + 2 * HEAD] = whole[edge : edge + tokens]
            gdown_ref[:, base : base + 2 * HEAD] = whole[edge + tokens :].astype(bf16)


def weight_copies(core, own_ref, other_ref, merge_buf, low_buf, sems):
    merge_rows = merge_buf.shape[1]
    low_rows = low_buf.shape[2]
    half = own_ref.shape[2]
    here = pl.multiple_of(core * half, 128)
    there = pl.multiple_of((1 - core) * half, 128)
    merge, low = [], []
    for side, (ref, place) in enumerate(((own_ref, here), (other_ref, there))):
        merge.append(
            pltpu.make_async_copy(
                ref.at[:, 0:merge_rows, :],
                merge_buf.at[:, :, pl.ds(place, half)],
                sems.at[4 * side],
            )
        )
    for block in range(3):
        at = merge_rows + block * low_rows
        for side, (ref, place) in enumerate(((own_ref, here), (other_ref, there))):
            low.append(
                pltpu.make_async_copy(
                    ref.at[:, at : at + low_rows, :],
                    low_buf.at[block, :, :, pl.ds(place, half)],
                    sems.at[4 * side + 1 + block],
                )
            )
    return merge, low


def flat(ref_value):
    return ref_value.reshape(ref_value.shape[0] * ref_value.shape[1], ref_value.shape[2])


def low_forward(
    pos_ref, unsh_ref, cond_ref, cot_ref, own_ref, other_ref,
    low_ref, normed_ref, send_ref, merge_buf, low_buf, sems,
):
    merge, lower = weight_copies(pos_ref[1], own_ref, other_ref, merge_buf, low_buf, sems)
    for copy in merge + lower:
        copy.start()
    for copy in merge:
        copy.wait()
    low = dot_nn(unsh_ref[...], flat(merge_buf[...])).astype(bf16)
    low_ref[...] = low
    low = low.astype(f32)
    normed = (low * unit_scale(low) * cond_ref[...]).astype(bf16)
    normed_ref[...] = normed
    parts = []
    for block in range(3):
        lower[2 * block].wait()
        lower[2 * block + 1].wait()
        parts.append(dot_nn(normed, flat(low_buf[block])).astype(bf16))
    query, key, value = parts
    cot = cot_ref[...]
    tokens = query.shape[0]
    share = tokens // 2
    for head in range(query.shape[1] // HEAD):
        at = head * HEAD
        key_value = jnp.concatenate([key[:, at : at + HEAD], value[:, at : at + HEAD]], axis=1)
        query_grad = jnp.concatenate([query[:, at : at + HEAD], cot[:, at : at + HEAD]], axis=1)
        for part in range(2):
            send_ref[2 * head + part, 0:tokens, :] = key_value
            send_ref[2 * head + part, tokens:, :] = query_grad[part * share : (part + 1) * share]


def low_attend(pos_ref, scale_ref, recv_ref, back_ref, key_s, key_t_s, wide_s, wide_t_s, gk_s, gv_s):
    gain = scale_ref[pos_ref[2]] * (1.0 / HEAD)
    sources = recv_ref.shape[0]
    tokens = recv_ref.shape[1] * 2 // 3
    share = tokens // 2
    keys = sources * tokens
    both = recv_ref[:, 0:tokens, :].reshape(keys, 2 * HEAD)
    key = both[:, :HEAD].astype(f32)
    key_scale = unit_scale(key)
    key_f = key * key_scale
    key_s[...] = key_f.astype(bf16)
    key_t_s[...] = jnp.concatenate([key_f, jnp.zeros_like(key_f)], axis=1).T.astype(bf16)
    wide = jnp.concatenate([both[:, HEAD:].astype(f32), jnp.ones_like(key_f)], axis=1)
    wide_s[...] = wide.astype(bf16)
    wide_t_s[...] = wide.T.astype(bf16)
    group = 8
    rows = group * share
    for block in range(sources // group):
        item = recv_ref[block * group : (block + 1) * group, tokens:, :].reshape(rows, 2 * HEAD)
        item = item.astype(f32)
        query, cot = item[:, :HEAD], item[:, HEAD:]
        query_scale = unit_scale(query)
        query_unit = (query * (query_scale * (gain * log2e))).astype(bf16)
        weight = jnp.exp2(dot_nt(key_s[...], query_unit)).astype(bf16)
        total = dot_nn(wide_t_s[...], weight).T
        inverse = 1.0 / total[:, HEAD:]
        out = total[:, :HEAD] * inverse
        grad = grad_ext(cot * inverse, out)
        slope = (weight.astype(f32) * dot_nt(wide_s[...], grad)).astype(bf16)
        gv = dot_nn(weight, grad)
        gk = dot_nn(slope, query_unit)
        if block == 0:
            gv_s[...] = gv
            gk_s[...] = gk
        else:
            gv_s[...] += gv
            gk_s[...] += gk
        gq = dot_nn(key_t_s[...], slope).T[:, :HEAD] * gain
        gq = unit_pull(query, query_scale, gq)
        result = jnp.concatenate([out, gq], axis=1).astype(bf16)
        back_ref[block * group : (block + 1) * group, tokens:, :] = result.reshape(
            group, share, 2 * HEAD
        )
    gk = unit_pull(key, key_scale, gk_s[...] * (1.0 / log2e))
    result = jnp.concatenate([gk, gv_s[:, :HEAD]], axis=1).astype(bf16)
    back_ref[:, 0:tokens, :] = result.reshape(sources, tokens, 2 * HEAD)


def low_backward(
    pos_ref, ret_ref, low_ref, cond_ref, cot_ref, own_ref, other_ref,
    output_ref, glp_ref, glow_ref, gmid_ref, proj_s, merge_buf, low_buf, sems,
):
    merge, lower = weight_copies(pos_ref[1], own_ref, other_ref, merge_buf, low_buf, sems)
    for copy in lower + merge:
        copy.start()
    tokens, width = low_ref.shape
    share = tokens // 2
    low = low_ref[...].astype(f32)
    for pair in range(width // (2 * HEAD)):
        outs, gqs, gks, gvs = [], [], [], []
        for head in (2 * pair, 2 * pair + 1):
            first, second = ret_ref[2 * head], ret_ref[2 * head + 1]
            sums = first[:tokens].astype(f32) + second[:tokens].astype(f32)
            gks.append(sums[:, :HEAD])
            gvs.append(sums[:, HEAD:])
            query = jnp.concatenate([first[tokens:], second[tokens:]], axis=0)
            outs.append(query[:, :HEAD])
            gqs.append(query[:, HEAD:])
        at = pair * 2 * HEAD
        out = jnp.concatenate(outs, axis=1).astype(f32)
        output_ref[:, at : at + 2 * HEAD] = (low[:, at : at + 2 * HEAD] + out).astype(bf16)
        proj_s[:, at : at + 2 * HEAD] = jnp.concatenate(gqs, axis=1)
        proj_s[:, width + at : width + at + 2 * HEAD] = jnp.concatenate(gks, axis=1).astype(bf16)
        proj_s[:, 2 * width + at : 2 * width + at + 2 * HEAD] = jnp.concatenate(
            gvs, axis=1
        ).astype(bf16)
    groups, _, share_cols = glp_ref.shape
    for part in range(groups):
        glp_ref[part] = proj_s[:, part * share_cols : (part + 1) * share_cols]
    back = jnp.zeros((tokens, width), f32)
    for block in range(3):
        lower[2 * block].wait()
        lower[2 * block + 1].wait()
        back = back + dot_nt(proj_s[:, block * width : (block + 1) * width], flat(low_buf[block]))
    grad = unit_pull(low, unit_scale(low), back * cond_ref[...])
    grad = (cot_ref[...].astype(f32) + grad).astype(bf16)
    share_cols = glow_ref.shape[2]
    for part in range(groups):
        glow_ref[part] = grad[:, part * share_cols : (part + 1) * share_cols]
    for copy in merge:
        copy.wait()
    wide = dot_nt(grad, flat(merge_buf[...]))
    top = gmid_ref.shape[1]
    half = 16
    for row in range(2 * tokens // half):
        for odd in range(2):
            at = (2 * row + odd) * half
            low_at = (row // 2) * half
            place = (2 * (row % 2) + odd) * top
            gmid_ref[at : at + half, :] = wide[low_at : low_at + half, place : place + top]


def gather_top_grads(gq_ref, gmid_ref, prev_ref, next_ref, whole_ref, parts_ref):
    tokens, top = gq_ref.shape
    edge = prev_ref.shape[0]
    whole_ref[:, :top] = gq_ref[...]
    whole_ref[0:edge, top:] = (gmid_ref[0:edge] + prev_ref[...].astype(f32)).astype(bf16)
    whole_ref[edge : tokens - edge, top:] = gmid_ref[edge : tokens - edge].astype(bf16)
    whole_ref[tokens - edge :, top:] = (
        gmid_ref[tokens - edge :] + next_ref[...].astype(f32)
    ).astype(bf16)
    groups, _, cols = parts_ref.shape
    for part in range(groups):
        parts_ref[part] = whole_ref[:, part * cols : (part + 1) * cols]


def finish_tokens(pos_ref, whole_ref, tok_ref, cond_ref, grad_ref, own_ref, other_ref, out_ref):
    core = pos_ref[1]
    width = own_ref.shape[1]
    here = pl.multiple_of(core * width, 128)
    there = pl.multiple_of((1 - core) * width, 128)
    back = dot_nt(whole_ref[:, pl.ds(here, width)], own_ref[...])
    back = back + dot_nt(whole_ref[:, pl.ds(there, width)], other_ref[...])
    tok = tok_ref[...].astype(f32)
    out_ref[...] = (
        grad_ref[...] + unit_pull(tok, unit_scale(tok), back * cond_ref[...])
    ).astype(bf16)


def to_all(block, axis):
    return lax.all_to_all(block, axis, split_axis=0, concat_axis=0, tiled=True)


def spread(block, axis):
    count = lax.axis_size(axis)
    return lax.all_to_all(
        jnp.broadcast_to(block[None], (count,) + block.shape), axis, split_axis=0, concat_axis=0
    )


def swap_cores(block):
    return lax.ppermute(block, "c", [(0, 1), (1, 0)])


def body(
    image_tokens,
    top_cond,
    bottom_cond,
    top_qkv,
    top_scale,
    merge_weight,
    bottom_qkv,
    bottom_scale,
    out_cotangent,
):
    _, shard_rows, cols, top = image_tokens.shape
    width = bottom_cond.shape[1]
    row_devices = lax.axis_size(ROWS)
    images = lax.axis_size(DP)
    grid_rows = shard_rows * row_devices
    tokens = shard_rows * cols
    low_tokens = tokens // 4
    edge = 3 * cols
    row_at = lax.axis_index(ROWS)
    core = lax.axis_index("c")
    pos = jnp.stack([row_at * shard_rows, core, row_at // 2]).astype(jnp.int32)

    low_rows = bottom_qkv.shape[0]
    merge_rows = merge_weight.shape[0]
    pack_rows = merge_rows + 3 * low_rows
    packed = jnp.concatenate(
        [merge_weight] + [bottom_qkv[:, i * width : (i + 1) * width] for i in range(3)], axis=0
    )
    packed = lax.dynamic_slice_in_dim(packed, core * (width // 2), width // 2, 1)
    w_own = lax.all_gather(packed, ROWS, axis=0, tiled=False)
    w_other = swap_cores(w_own)
    top_half = top_qkv.shape[1] // 2
    top_piece = lax.dynamic_slice_in_dim(top_qkv, core * top_half, top_half, 1)
    top_own = spread(spread(top_piece, "z"), "x").reshape(top, top_half)
    top_other = swap_cores(top_own)

    tok = image_tokens[0].reshape(shard_rows, cols // 2, 2, top).transpose(0, 2, 1, 3)
    tok = tok.reshape(tokens, top)
    tok_f = tok.astype(f32)
    top_flat = (tok_f * unit_scale(tok_f) * top_cond[0]).astype(bf16)
    proj, up, down = call(
        project_top,
        [smem(), vmem(), vmem(), vmem()],
        [((tokens, 3 * top), bf16), ((edge, 2 * top), bf16), ((edge, 2 * top), bf16)],
        name="project_top",
    )(pos, top_flat, top_own, top_other)
    forward = [(i, i + 1) for i in range(row_devices - 1)]
    backward = [(i + 1, i) for i in range(row_devices - 1)]
    lo = lax.ppermute(down, ROWS, forward)
    hi = lax.ppermute(up, ROWS, backward)
    unshuffled, top_out, top_inv = call(
        functools.partial(top_forward, grid_rows, cols),
        [smem(), smem()] + [vmem()] * 4,
        [((low_tokens, 4 * top), bf16), ((tokens, top), f32), ((tokens, top), f32)],
        [pltpu.VMEM((tokens, tokens + 2 * edge), f32)],
        name="top_forward",
    )(pos, top_scale, tok, proj, lo, hi)

    cot = out_cotangent[0].reshape(low_tokens, width)
    weight_scratch = [
        pltpu.VMEM((row_devices, merge_rows, width), bf16),
        pltpu.VMEM((3, row_devices, low_rows, width), bf16),
        pltpu.SemaphoreType.DMA((8,)),
    ]
    exchange = (row_devices, low_tokens * 3 // 2, 2 * HEAD)
    low, low_normed, send = call(
        low_forward,
        [smem()] + [vmem()] * 3 + [anywhere()] * 2,
        [((low_tokens, width), bf16), ((low_tokens, width), bf16), (exchange, bf16)],
        weight_scratch,
        name="low_forward",
    )(pos, unshuffled, bottom_cond, cot, w_own, w_other)
    recv = to_all(send, ROWS)
    keys = row_devices * low_tokens
    (back,) = call(
        low_attend,
        [smem(), smem(), vmem()],
        [(exchange, bf16)],
        [
            pltpu.VMEM((keys, HEAD), bf16),
            pltpu.VMEM((2 * HEAD, keys), bf16),
            pltpu.VMEM((keys, 2 * HEAD), bf16),
            pltpu.VMEM((2 * HEAD, keys), bf16),
            pltpu.VMEM((keys, HEAD), f32),
            pltpu.VMEM((keys, 2 * HEAD), f32),
        ],
        name="low_attend",
    )(pos, bottom_scale, recv)
    ret = to_all(back, ROWS)
    output, grad_proj, grad_low, grad_middle = call(
        low_backward,
        [smem()] + [vmem()] * 4 + [anywhere()] * 2,
        [
            ((low_tokens, width), bf16),
            ((images, low_tokens, 3 * width // images), bf16),
            ((images, low_tokens, width // images), bf16),
            ((tokens, top), f32),
        ],
        [pltpu.VMEM((low_tokens, 3 * width), bf16)] + weight_scratch,
        name="low_backward",
    )(pos, ret, low, bottom_cond, cot, w_own, w_other)

    gq, gmid, gup, gdown = call(
        functools.partial(top_backward, grid_rows, cols),
        [smem(), smem()] + [vmem()] * 6,
        [
            ((tokens, top), bf16),
            ((tokens, 2 * top), f32),
            ((edge, 2 * top), bf16),
            ((edge, 2 * top), bf16),
        ],
        [pltpu.VMEM((tokens + 2 * edge, tokens), f32)],
        name="top_backward",
    )(pos, top_scale, proj, lo, hi, top_out, top_inv, grad_middle)
    from_next = lax.ppermute(gup, ROWS, backward)
    from_prev = lax.ppermute(gdown, ROWS, forward)
    grad_top, grad_top_parts = call(
        gather_top_grads,
        [vmem()] * 4,
        [((tokens, 3 * top), bf16), ((images, tokens, 3 * top // images), bf16)],
        name="gather_top_grads",
    )(gq, gmid, from_prev, from_next)
    (grad_tokens,) = call(
        finish_tokens,
        [smem()] + [vmem()] * 6,
        [((tokens, top), bf16)],
        name="finish_tokens",
    )(pos, grad_top, tok, top_cond, grad_middle, top_own, top_other)

    top_flat_late, _ = lax.optimization_barrier((top_flat, w_own))
    top_all = lax.all_gather(top_flat_late, DP, axis=0, tiled=True)
    unsh_all = lax.all_gather(unshuffled, DP, axis=0, tiled=True)
    normed_all = lax.all_gather(low_normed, DP, axis=0, tiled=True)
    proj_all = to_all(grad_proj, DP).reshape(images * low_tokens, 3 * width // images)
    glow_all = to_all(grad_low, DP).reshape(images * low_tokens, width // images)
    part_low = dot_tn(normed_all, proj_all).astype(bf16)
    part_merge = dot_tn(unsh_all, glow_all).astype(bf16)
    pieces = part_low.shape[1] // 128
    part_low = part_low.reshape(row_devices, low_rows, pieces, 128).transpose(0, 2, 1, 3)
    part_low = part_low.reshape(row_devices, pieces * low_rows, 128)
    part_merge = part_merge.reshape(row_devices, merge_rows, 128)
    sums = to_all(jnp.concatenate([part_merge, part_low], axis=1), ROWS)
    sums = jnp.sum(sums.astype(f32), axis=0)
    sum_merge = sums[:merge_rows]
    sum_low = sums[merge_rows:].reshape(pieces, low_rows, 128).transpose(1, 0, 2)
    sum_low = sum_low.reshape(low_rows, pieces * 128)
    top_cols = 3 * top // images
    parts_all = to_all(grad_top_parts, DP).reshape(images * tokens, top_cols)
    part_top = dot_tn(top_all, parts_all).astype(bf16)
    part_top = to_all(part_top.reshape(row_devices, top // row_devices, top_cols), ROWS)
    sum_top = jnp.sum(part_top.astype(f32), axis=0)

    grad_tokens = grad_tokens.reshape(shard_rows, 2, cols // 2, top).transpose(0, 2, 1, 3)
    return (
        output.reshape(1, shard_rows // 2, cols // 2, width),
        grad_tokens.reshape(1, shard_rows, cols, top),
        sum_top,
        sum_merge,
        sum_low,
    )


def solution(mesh):
    images, row_devices = mesh.shape["dp"], mesh.shape["rows"]
    grid = mesh.devices.reshape(images // 2, 2, row_devices // 8, 8)
    split = Mesh(grid, ("y", "c", "x", "z"))
    placed = (
        P(DP, ROWS, None, None),
        P(DP, None),
        P(DP, None),
        P(ROWS, None),
        P(),
        P(ROWS, None),
        P(ROWS, None),
        P(),
        P(DP, ROWS, None, None),
    )
    return jax.shard_map(
        body,
        mesh=split,
        in_specs=placed,
        out_specs=(
            P(DP, ROWS, None, None),
            P(DP, ROWS, None, None),
            P(ROWS, DP),
            P(ROWS, DP),
            P(ROWS, DP),
        ),
        check_vma=False,
    )
```

time: 1450 us -> 339 us (0.23)
  waiting for transfers between devices: 882 us -> 114 us
  other arithmetic: 312 us -> 5.2 us
  local copies, waits for them, and re-layouts: 113 us -> 23.2 us
  blocking collectives: 0 us -> 79.3 us
  Pallas kernels: 0 us -> 44 us
  matrix products: 50.3 us -> 8.3 us
  loops' own time: 26.5 us -> 0 us
    reduce_scatter x3 -> x0, waiting for transfers between devices: 650 us -> none  [the longest x1 224 us: body(): lax.psum_scatter(part_low.astype(jnp.bfloat16), 'rows', scatter_dimension...]
    unnamed x12 -> x4, waiting for transfers between devices: 101 us -> 0.85 us
    mul x39 -> x0, other arithmetic: 91.2 us -> none  [the longest x21 46.3 us: one_row(): score = scales * jnp.mean(query_unit * key_part, axis=-1)]
    all_to_all x0 -> x4, blocking collectives: none -> 79.3 us  [the longest x2 45.5 us: to_all(): return lax.all_to_all(block, axis, split_axis=0, concat_axis=0, tiled=True)]
    add x23 -> x0, other arithmetic: 65.1 us -> none  [the longest x7 45.3 us: one_row(): numer = numer + weight[..., None] * value_part]
    reduce_sum x24 -> x3, other arithmetic: 55.8 us -> 2.31 us  [the longest x1 1.51 us: body(): sums = jnp.sum(sums.astype(f32), axis=0)]
    all_gather x3 -> x4, waiting for transfers between devices: 107 us -> 54.1 us  [the longest x1 54.1 us: body(): w_own = lax.all_gather(packed, ROWS, axis=0, tiled=False)]
    pallas_call x0 -> x8, Pallas kernels: none -> 44 us  [the longest x1 12.9 us: body(): call(functools.partial(top_backward, grid_rows, cols), [smem(), smem()] +...]
  transfers between devices with their start and end apart: 17 -> 15, of which waited for: 14 -> 9; matrix products, arithmetic and copies ran while one was open for 12% -> 5% of each run, Pallas kernels for 0% -> 13%
where the time goes in v1:
time: 339 us; the launch traced here: 336 us
  waiting for transfers between devices  114 us (34%)
  blocking collectives  79.3 us (23%)
  starting transfers between devices  45.7 us (13%)
  Pallas kernels  44 us (13%)
  local copies, waits for them, and re-layouts  23.2 us (7%)
  between operations  16.1 us (5%)
  matrix products  8.3 us (2%)
  other arithmetic  5.2 us (2%)
    all_to_all x5, waiting for transfers between devices, to_all(): return lax.all_to_all(block, axis, split_axis=0, concat_axis=0, tiled=True)  54.2 us
    all_gather x1, waiting for transfers between devices, body(): w_own = lax.all_gather(packed, ROWS, axis=0, tiled=False)  54.1 us
    all_to_all x2, blocking collectives, to_all(): return lax.all_to_all(block, axis, split_axis=0, concat_axis=0, tiled=True)  45.5 us
    all_to_all x2, blocking collectives, spread(): lax.all_to_all(jnp.broadcast_to(block[None], (count,) + block.shape), axi...  33.8 us
    all_to_all x5, starting transfers between devices, to_all(): return lax.all_to_all(block, axis, split_axis=0, concat_axis=0, tiled=True)  29.4 us
    unnamed x65, local copies, waits for them, and re-layouts  15.5 us
    pallas_call x1, Pallas kernels, body(): call(functools.partial(top_backward, grid_rows, cols), [smem(), smem()] +...  12.9 us
    pallas_call x1, Pallas kernels, body(): call(low_attend, [smem(), smem(), vmem()], [(exchange, bf16)], [pltpu.VME...  11.2 us
  transfers between devices with their start and end apart: 15, of which 9 were waited for; matrix products, arithmetic and copies ran while one was open for 5% of the time, Pallas kernels for 13%

profile of v1, /device:TPU:2, one launch (start us, length us, event | category | flops | bytes accessed | tf_op | source)
XLA Modules:
  0.0 335.6 jit_solution(16582981459430382112)
XLA Ops:
  9.0 1.5 fusion.2
  10.7 18.7 %all_to_all.45 = bf16[8,16,768]{2,1,0:T(8,128)(2,1)S(1)} all-to-all(bf16[8,16,768]{2,1,0:T(8,128)(2,1)S(1)} %broadcast_in_dim.4), channel_id=1, replica_groups=mesh['y'=4,'c'=2,'x'=4,'z'=8] {'z'}, dimensions={0} | all-to-all | bytes 393216 | tf_op jit(solution)/shard_map/all_to_all | solution.py:393
  29.5 15.0 %all_to_all.46 = bf16[4,8,16,768]{3,2,1,0:T(8,128)(2,1)S(1)} all-to-all(bf16[4,8,16,768]{3,2,1,0:T(8,128)(2,1)S(1)} %broadcast_in_dim.5), channel_id=1, replica_groups=mesh['y'=4,'c'=2,'x'=4,'z'=8] {'x'}, dimensions={0} | all-to-all | bytes 1572864 | tf_op jit(solution)/shard_map/all_to_all | solution.py:393
  44.8 54.1 %all-gather.12.cloned.1.call-done = bf16[5120,512]{1,0:T(8,128)(2,1)} async-done(((bf16[160,512]{1,0:T(8,128)(2,1)}), bf16[5120,512]{1,0:T(8,128)(2,1)}) %all-gather.12.cloned.1.call-update) | async-done | bytes 5242896 | tf_op jit(solution)/shard_map/all_gather | solution.py:432
  100.4 3.5 %collective-permute-start.1 = (bf16[96,1024]{1,0:T(8,128)(2,1)S(1)}, bf16[96,1024]{1,0:T(8,128)(2,1)S(1)}, u32[]{:S(2)}, u32[]{:S(2)}) collective-permute-start(bf16[96,1024]{1,0:T(8,128)(2,1)S(1)} %get-tuple-element.26), channel_id=1, source_target_pairs={{0,1},{1,2},{2,3},{3,4},{4,5},{5,6},{6,7},{7,8},{8,9},{9,10},{10,1... | collective-permute-start | bytes 589832 | tf_op jit(solution)/shard_map/ppermute | solution.py:451
  103.9 4.4 %collective-permute-start.2 = (bf16[96,1024]{1,0:T(8,128)(2,1)S(1)}, bf16[96,1024]{1,0:T(8,128)(2,1)S(1)}, u32[]{:S(2)}, u32[]{:S(2)}) collective-permute-start(bf16[96,1024]{1,0:T(8,128)(2,1)S(1)} %get-tuple-element.27), channel_id=1, source_target_pairs={{1,0},{2,1},{3,2},{4,3},{5,4},{6,5},{7,6},{8,7},{9,8},{10,9},{11,1... | collective-permute-start | bytes 589832 | tf_op jit(solution)/shard_map/ppermute | solution.py:452
  108.4 3.3 collective-permute-done.1.lo_ref
  112.9 5.9 %top_forward.1 = (bf16[64,2048]{1,0:T(8,128)(2,1)}, f32[256,512]{1,0:T(8,128)S(1)}, f32[256,512]{1,0:T(8,128)S(1)}) custom-call(s32[3]{0:T(128)S(1)} %pad_add_fusion.pos_ref, f32[8]{0:T(128)S(1)} %copy-done.28, bf16[256,512]{1,0:T(8,128)(2,1)S(1)} %bitcast.44, bf16[256,1536]{1,0:T(8,128)(2,1)S(1)} %get-tuple-element.25.proj_ref, ...), custom_call_target="tpu_custom_call" | custom-call | tf_op jit(solution)/shard_map/top_forward/pallas_call | solution.py:453
  121.8 2.5 copy-done.1
  124.2 5.5 %low_forward.1 = (bf16[64,1024]{1,0:T(8,128)(2,1)S(1)}, bf16[64,1024]{1,0:T(8,128)(2,1)S(1)}, bf16[32,96,128]{2,1,0:T(8,128)(2,1)S(1)}) custom-call(s32[3]{0:T(128)S(1)} %pad_add_fusion.pos_ref, bf16[64,2048]{1,0:T(8,128)(2,1)} %get-tuple-element.28.unsh_ref, f32[1,1024]{1,0:T(1,128)S(1)} %copy-done.26, bf16[64,1024]{1,0:T(8,128)(2,1)S(1)} %bitcast.47, ...), custom_call_target="tpu_custom_call" | custom-call | tf_op jit(solution)/shard_map/low_forward/pallas_call | solution.py:468
  129.7 28.4 %all_to_all.47.recv_ref = bf16[32,96,128]{2,1,0:T(8,128)(2,1)S(1)} all-to-all(bf16[32,96,128]{2,1,0:T(8,128)(2,1)S(1)} %get-tuple-element.29), channel_id=1, replica_groups=mesh['y'=4,'c'=2,'x'=4,'z'=8] {'x','z'}, dimensions={0} | all-to-all | bytes 1572864 | tf_op jit(solution)/shard_map/all_to_all | solution.py:388
  158.1 11.2 %low_attend.1 = bf16[32,96,128]{2,1,0:T(8,128)(2,1)} custom-call(s32[3]{0:T(128)S(1)} %pad_add_fusion.pos_ref, f32[16]{0:T(128)S(1)} %copy-done.29, bf16[32,96,128]{2,1,0:T(8,128)(2,1)S(1)} %all_to_all.47.recv_ref), custom_call_target="tpu_custom_call" | custom-call | tf_op jit(solution)/shard_map/low_attend/pallas_call | solution.py:477
  169.3 7.2 %all-to-all-start.3 = ((bf16[32,96,128]{2,1,0:T(8,128)(2,1)}), bf16[32,96,128]{2,1,0:T(8,128)(2,1)S(1)}, u32[]{:S(2)}, u32[]{:S(2)}) async-start(bf16[32,96,128]{2,1,0:T(8,128)(2,1)} %low_attend.1), calls=%async_computation.3 | async-start | bytes 1572864 | tf_op jit(solution)/shard_map/all_to_all | solution.py:388
  177.1 19.4 %all-to-all-done.3.ret_ref = bf16[32,96,128]{2,1,0:T(8,128)(2,1)S(1)} async-done(((bf16[32,96,128]{2,1,0:T(8,128)(2,1)}), bf16[32,96,128]{2,1,0:T(8,128)(2,1)S(1)}, u32[]{:S(2)}, u32[]{:S(2)}) %all-to-all-start.3) | async-done | bytes 786464 | tf_op jit(solution)/shard_map/all_to_all | solution.py:388
  196.5 2.6 copy-done.2
  200.9 5.9 %low_backward.1 = (bf16[64,1024]{1,0:T(8,128)(2,1)}, bf16[8,64,384]{2,1,0:T(8,128)(2,1)}, bf16[8,64,128]{2,1,0:T(8,128)(2,1)S(1)}, f32[256,512]{1,0:T(8,128)S(1)}) custom-call(s32[3]{0:T(128)S(1)} %pad_add_fusion.pos_ref, bf16[32,96,128]{2,1,0:T(8,128)(2,1)S(1)} %all-to-all-done.3.ret_ref, bf16[64,1024]{1,0:T(8,128)(2,1)S(1)} %copy-done.23, ...), custom_call_target="tpu_custom_call" | custom-call | tf_op jit(solution)/shard_map/low_backward/pallas_call | solution.py:492
  206.9 12.9 %top_backward.1 = (bf16[256,512]{1,0:T(8,128)(2,1)S(1)}, f32[256,1024]{1,0:T(8,128)S(1)}, bf16[96,1024]{1,0:T(8,128)(2,1)S(1)}, bf16[96,1024]{1,0:T(8,128)(2,1)}) custom-call(s32[3]{0:T(128)S(1)} %pad_add_fusion.pos_ref, f32[8]{0:T(128)S(1)} %copy-done.28, bf16[256,1536]{1,0:T(8,128)(2,1)S(1)} %get-tuple-element.25.proj_ref, bf16[96,1024]{1,0:T(8,128)(2,1)S(1)} %copy-done.9, ...), custom_call_target="tpu_custom_call" | custom-call | tf_op jit(solution)/shard_map/top_backward/pallas_call | solution.py:505
  220.8 4.8 %collective-permute-start.4 = (bf16[96,1024]{1,0:T(8,128)(2,1)}, bf16[96,1024]{1,0:T(8,128)(2,1)S(1)}, u32[]{:S(2)}, u32[]{:S(2)}) collective-permute-start(bf16[96,1024]{1,0:T(8,128)(2,1)} %get-tuple-element.37), channel_id=1, source_target_pairs={{0,1},{1,2},{2,3},{3,4},{4,5},{5,6},{6,7},{7,8},{8,9},{9,10},{10,1... | collective-permute-start | bytes 589832 | tf_op jit(solution)/shard_map/ppermute | solution.py:518
  225.6 3.2 collective-permute-start.5
  228.8 4.3 %all-to-all-start.6 = ((bf16[8,64,128]{2,1,0:T(8,128)(2,1)}), bf16[8,64,128]{2,1,0:T(8,128)(2,1)}, u32[]{:S(2)}, u32[]{:S(2)}) async-start(bf16[8,64,128]{2,1,0:T(8,128)(2,1)} %copy-done.25), calls=%async_computation.6 | async-start | bytes 262144 | tf_op jit(solution)/shard_map/all_to_all | solution.py:388
  239.3 17.1 %all_to_all.48 = bf16[8,256,192]{1,2,0:T(8,128)(2,1)S(1)} all-to-all(bf16[8,256,192]{1,2,0:T(8,128)(2,1)} %copy.30), channel_id=1, replica_groups=mesh['y'=4,'c'=2,'x'=4,'z'=8] {'y','c'}, dimensions={0} | all-to-all | bytes 1572864 | tf_op jit(solution)/shard_map/all_to_all | solution.py:388
  256.4 4.1 %all-to-all-start.7 = ((bf16[8,64,384]{2,1,0:T(8,128)(2,1)}), bf16[8,64,384]{2,1,0:T(8,128)(2,1)}, u32[]{:S(2)}, u32[]{:S(2)}) async-start(bf16[8,64,384]{2,1,0:T(8,128)(2,1)} %get-tuple-element.44), calls=%async_computation.7 | async-start | bytes 786432 | tf_op jit(solution)/shard_map/all_to_all | solution.py:388
  260.5 3.2 convolution_convert_fusion
  263.8 2.2 convolution_convert_fusion.2
  266.8 2.6 all-to-all-done.7
  269.4 7.3 %all-to-all-start.5 = ((bf16[32,16,192]{2,1,0:T(8,128)(2,1)}), bf16[32,16,192]{2,1,0:T(8,128)(2,1)S(1)}, u32[]{:S(2)}, u32[]{:S(2)}) async-start(bf16[32,16,192]{2,1,0:T(8,128)(2,1)} %bitcast.13), calls=%async_computation.5 | async-start | bytes 524288 | tf_op jit(solution)/shard_map/all_to_all | solution.py:388
  276.8 3.0 convolution_convert_fusion.1
  279.8 2.4 reshape.81
  284.4 3.4 %all-to-all-done.5 = bf16[32,16,192]{2,1,0:T(8,128)(2,1)S(1)} async-done(((bf16[32,16,192]{2,1,0:T(8,128)(2,1)}), bf16[32,16,192]{2,1,0:T(8,128)(2,1)S(1)}, u32[]{:S(2)}, u32[]{:S(2)}) %all-to-all-start.5) | async-done | bytes 196640 | tf_op jit(solution)/shard_map/all_to_all | solution.py:388
  287.7 6.5 %all-to-all-start.8 = ((bf16[32,160,128]{2,1,0:T(8,128)(2,1)}), bf16[32,160,128]{2,1,0:T(8,128)(2,1)}, u32[]{:S(2)}, u32[]{:S(2)}) async-start(bf16[32,160,128]{2,1,0:T(8,128)(2,1)} %pad_maximum_fusion), calls=%async_computation.8 | async-start | bytes 2621440 | tf_op jit(solution)/shard_map/all_to_all | solution.py:388
  297.2 28.0 %all-to-all-done.8 = bf16[32,160,128]{2,1,0:T(8,128)(2,1)} async-done(((bf16[32,160,128]{2,1,0:T(8,128)(2,1)}), bf16[32,160,128]{2,1,0:T(8,128)(2,1)}, u32[]{:S(2)}, u32[]{:S(2)}) %all-to-all-start.8) | async-done | bytes 1310752 | tf_op jit(solution)/shard_map/all_to_all | solution.py:388
  325.2 1.5 convert_reduce_fusion
  (107 shorter events, 24.0 us)
Async XLA Ops:
  8.0 90.9 %all-gather.12.cloned.1.call-start = ((), (), s32[]{:S(2)}) async-start(), calls=%async_computation.12 | async-start | bytes 5406720 | tf_op jit(solution)/shard_map/all_gather | solution.py:432
  8.1 36.5 %copy-start.31 = (bf16[1,8,32,512]{3,2,1,0:T(8,128)(2,1)S(1)}, bf16[1,8,32,512]{3,2,1,0:T(8,128)(2,1)}, u32[]{:S(2)}) copy-start(bf16[1,8,32,512]{3,2,1,0:T(8,128)(2,1)} %param.9) | copy-start | bytes 786436
  10.6 249.9 %all-gather.8.cloned.1.call-start = ((), (), s32[]{:S(2)}) async-start(), calls=%async_computation.10 | async-start | bytes 2359296 | tf_op jit(solution)/shard_map/all_gather | solution.py:534
  10.7 88.4 %copy-start.27 = (f32[1,512]{1,0:T(1,128)S(1)}, f32[1,512]{1,0:T(1,128)}, u32[]{:S(2)}) copy-start(f32[1,512]{1,0:T(1,128)} %cond_ref.5) | copy-start | bytes 6148
  44.6 68.4 %copy-start.28 = (f32[8]{0:T(128)S(1)}, f32[8]{0:T(128)}, u32[]{:S(2)}) copy-start(f32[8]{0:T(128)} %scale_ref.5) | copy-start | bytes 100
  44.6 54.7 %collective-permute-start = (bf16[512,768]{1,0:T(8,128)(2,1)S(1)}, bf16[512,768]{1,0:T(8,128)(2,1)S(1)}, u32[]{:S(2)}, u32[]{:S(2)}) collective-permute-start(bf16[512,768]{1,0:T(8,128)(2,1)S(1)} %bitcast.41), channel_id=1, source_target_pairs={{0,32},{32,0},{1,33},{33,1},{2,34},{34,2},{3,35},{35,3},{4,36},{36... | collective-permute-start | bytes 2359304 | tf_op jit(solution)/shard_map/ppermute | solution.py:399
  98.9 22.8 %collective-permute-start.3 = (bf16[32,160,512]{2,1,0:T(8,128)(2,1)}, bf16[32,160,512]{2,1,0:T(8,128)(2,1)}, u32[]{:S(2)}, u32[]{:S(2)}) collective-permute-start(bf16[32,160,512]{2,1,0:T(8,128)(2,1)} %bitcast.38), channel_id=1, source_target_pairs={{0,32},{32,0},{1,33},{33,1},{2,34},{34,2},{3,35},{35,3},{4,36},{36... | collective-permute-start | bytes 15728648 | tf_op jit(solution)/shard_map/ppermute | solution.py:399
  99.1 22.6 %copy-start.14 = (bf16[1,4,16,1024]{3,2,1,0:T(8,128)(2,1)S(1)}, bf16[1,4,16,1024]{3,2,1,0:T(8,128)(2,1)}, u32[]{:S(2)}) copy-start(bf16[1,4,16,1024]{3,2,1,0:T(8,128)(2,1)} %param.17) | copy-start | bytes 393220
  99.1 22.6 %copy-start.26 = (f32[1,1024]{1,0:T(1,128)S(1)}, f32[1,1024]{1,0:T(1,128)}, u32[]{:S(2)}) copy-start(f32[1,1024]{1,0:T(1,128)} %cond_ref.4) | copy-start | bytes 12292
  99.3 21.9 %copy-start.3 = (bf16[256,512]{1,0:T(8,128)(2,1)}, bf16[256,512]{1,0:T(8,128)(2,1)S(1)}, u32[]{:S(2)}) copy-start(bf16[256,512]{1,0:T(8,128)(2,1)S(1)} %multiply_convert_fusion.flat_ref) | copy-start | bytes 786436
  100.4 11.3 %collective-permute-start.1 = (bf16[96,1024]{1,0:T(8,128)(2,1)S(1)}, bf16[96,1024]{1,0:T(8,128)(2,1)S(1)}, u32[]{:S(2)}, u32[]{:S(2)}) collective-permute-start(bf16[96,1024]{1,0:T(8,128)(2,1)S(1)} %get-tuple-element.26), channel_id=1, source_target_pairs={{0,1},{1,2},{2,3},{3,4},{4,5},{5,6},{6,7},{7,8},{8,9},{9,10},{10,1... | collective-permute-start | bytes 589832 | tf_op jit(solution)/shard_map/ppermute | solution.py:451
  103.9 9.0 %collective-permute-start.2 = (bf16[96,1024]{1,0:T(8,128)(2,1)S(1)}, bf16[96,1024]{1,0:T(8,128)(2,1)S(1)}, u32[]{:S(2)}, u32[]{:S(2)}) collective-permute-start(bf16[96,1024]{1,0:T(8,128)(2,1)S(1)} %get-tuple-element.27), channel_id=1, source_target_pairs={{1,0},{2,1},{3,2},{4,3},{5,4},{6,5},{7,6},{8,7},{9,8},{10,9},{11,1... | collective-permute-start | bytes 589832 | tf_op jit(solution)/shard_map/ppermute | solution.py:452
  121.1 142.7 %all-gather.6.cloned.1.call-start = ((), (), s32[]{:S(2)}) async-start(), calls=%async_computation.9 | async-start | bytes 2359296 | tf_op jit(solution)/shard_map/all_gather | solution.py:533
  124.2 33.9 %copy-start.29 = (f32[16]{0:T(128)S(1)}, f32[16]{0:T(128)}, u32[]{:S(2)}) copy-start(f32[16]{0:T(128)} %scale_ref.4) | copy-start | bytes 196
  129.7 28.4 %copy-start.22 = (bf16[64,1024]{1,0:T(8,128)(2,1)}, bf16[64,1024]{1,0:T(8,128)(2,1)S(1)}, u32[]{:S(2)}) copy-start(bf16[64,1024]{1,0:T(8,128)(2,1)S(1)} %get-tuple-element.30.low_ref) | copy-start | bytes 393220
  129.7 28.4 %copy-start.24 = (bf16[64,1024]{1,0:T(8,128)(2,1)}, bf16[64,1024]{1,0:T(8,128)(2,1)S(1)}, u32[]{:S(2)}) copy-start(bf16[64,1024]{1,0:T(8,128)(2,1)S(1)} %get-tuple-element.43) | copy-start | bytes 393220
  169.3 27.2 %all-to-all-start.3 = ((bf16[32,96,128]{2,1,0:T(8,128)(2,1)}), bf16[32,96,128]{2,1,0:T(8,128)(2,1)S(1)}, u32[]{:S(2)}, u32[]{:S(2)}) async-start(bf16[32,96,128]{2,1,0:T(8,128)(2,1)} %low_attend.1), calls=%async_computation.3 | async-start | bytes 1572864 | tf_op jit(solution)/shard_map/all_to_all | solution.py:388
  176.5 100.2 %all-gather.10.cloned.1.call-start = ((), (), s32[]{:S(2)}) async-start(), calls=%async_computation.11 | async-start | bytes 1179648 | tf_op jit(solution)/shard_map/all_gather | solution.py:535
  200.9 5.9 %copy-start.9 = (bf16[96,1024]{1,0:T(8,128)(2,1)S(1)}, bf16[96,1024]{1,0:T(8,128)(2,1)}, u32[]{:S(2)}) copy-start(bf16[96,1024]{1,0:T(8,128)(2,1)} %copy-done.8) | copy-start | bytes 589828
  200.9 6.0 %copy-start.11 = (bf16[96,1024]{1,0:T(8,128)(2,1)S(1)}, bf16[96,1024]{1,0:T(8,128)(2,1)}, u32[]{:S(2)}) copy-start(bf16[96,1024]{1,0:T(8,128)(2,1)} %copy-done.10) | copy-start | bytes 589828
  200.9 6.0 %copy-start.17 = (f32[256,512]{1,0:T(8,128)S(1)}, f32[256,512]{1,0:T(8,128)}, u32[]{:S(2)}) copy-start(f32[256,512]{1,0:T(8,128)} %copy-done.16) | copy-start | bytes 1572868
  200.9 6.0 %copy-start.19 = (f32[256,512]{1,0:T(8,128)S(1)}, f32[256,512]{1,0:T(8,128)}, u32[]{:S(2)}) copy-start(f32[256,512]{1,0:T(8,128)} %copy-done.18) | copy-start | bytes 1572868
  206.8 13.0 %copy-start.4 = (f32[256,512]{1,0:T(8,128)}, f32[256,512]{1,0:T(8,128)S(1)}, u32[]{:S(2)}) copy-start(f32[256,512]{1,0:T(8,128)S(1)} %get-tuple-element.34.grad_ref) | copy-start | bytes 1572868
  206.9 21.9 %copy-start.25 = (bf16[8,64,128]{2,1,0:T(8,128)(2,1)}, bf16[8,64,128]{2,1,0:T(8,128)(2,1)S(1)}, u32[]{:S(2)}) copy-start(bf16[8,64,128]{2,1,0:T(8,128)(2,1)S(1)} %get-tuple-element.42) | copy-start | bytes 393220
  220.8 12.2 %collective-permute-start.4 = (bf16[96,1024]{1,0:T(8,128)(2,1)}, bf16[96,1024]{1,0:T(8,128)(2,1)S(1)}, u32[]{:S(2)}, u32[]{:S(2)}) collective-permute-start(bf16[96,1024]{1,0:T(8,128)(2,1)} %get-tuple-element.37), channel_id=1, source_target_pairs={{0,1},{1,2},{2,3},{3,4},{4,5},{5,6},{6,7},{7,8},{8,9},{9,10},{10,1... | collective-permute-start | bytes 589832 | tf_op jit(solution)/shard_map/ppermute | solution.py:518
  225.6 7.6 %collective-permute-start.5 = (bf16[96,1024]{1,0:T(8,128)(2,1)S(1)}, bf16[96,1024]{1,0:T(8,128)(2,1)S(1)}, u32[]{:S(2)}, u32[]{:S(2)}) collective-permute-start(bf16[96,1024]{1,0:T(8,128)(2,1)S(1)} %get-tuple-element.38), channel_id=1, source_target_pairs={{1,0},{2,1},{3,2},{4,3},{5,4},{6,5},{7,6},{8,7},{9,8},{10,9},{11,1... | collective-permute-start | bytes 589832 | tf_op jit(solution)/shard_map/ppermute | solution.py:517
  228.8 10.5 %all-to-all-start.6 = ((bf16[8,64,128]{2,1,0:T(8,128)(2,1)}), bf16[8,64,128]{2,1,0:T(8,128)(2,1)}, u32[]{:S(2)}, u32[]{:S(2)}) async-start(bf16[8,64,128]{2,1,0:T(8,128)(2,1)} %copy-done.25), calls=%async_computation.6 | async-start | bytes 262144 | tf_op jit(solution)/shard_map/all_to_all | solution.py:388
  256.4 13.1 %all-to-all-start.7 = ((bf16[8,64,384]{2,1,0:T(8,128)(2,1)}), bf16[8,64,384]{2,1,0:T(8,128)(2,1)}, u32[]{:S(2)}, u32[]{:S(2)}) async-start(bf16[8,64,384]{2,1,0:T(8,128)(2,1)} %get-tuple-element.44), calls=%async_computation.7 | async-start | bytes 786432 | tf_op jit(solution)/shard_map/all_to_all | solution.py:388
  269.4 18.3 %all-to-all-start.5 = ((bf16[32,16,192]{2,1,0:T(8,128)(2,1)}), bf16[32,16,192]{2,1,0:T(8,128)(2,1)S(1)}, u32[]{:S(2)}, u32[]{:S(2)}) async-start(bf16[32,16,192]{2,1,0:T(8,128)(2,1)} %bitcast.13), calls=%async_computation.5 | async-start | bytes 524288 | tf_op jit(solution)/shard_map/all_to_all | solution.py:388
  283.2 11.0 %copy-start.5 = (f32[256,512]{1,0:T(8,128)S(1)}, f32[256,512]{1,0:T(8,128)}, u32[]{:S(2)}) copy-start(f32[256,512]{1,0:T(8,128)} %copy-done.4) | copy-start | bytes 1572868
  283.2 11.0 %copy-start.13 = (bf16[256,1536]{1,0:T(8,128)(2,1)S(1)}, bf16[256,1536]{1,0:T(8,128)(2,1)}, u32[]{:S(2)}) copy-start(bf16[256,1536]{1,0:T(8,128)(2,1)} %copy-done.12) | copy-start | bytes 2359300
  287.7 37.5 %all-to-all-start.8 = ((bf16[32,160,128]{2,1,0:T(8,128)(2,1)}), bf16[32,160,128]{2,1,0:T(8,128)(2,1)}, u32[]{:S(2)}, u32[]{:S(2)}) async-start(bf16[32,160,128]{2,1,0:T(8,128)(2,1)} %pad_maximum_fusion), calls=%async_computation.8 | async-start | bytes 2621440 | tf_op jit(solution)/shard_map/all_to_all | solution.py:388
  (15 other events, 23.5 us)
Sparse Core Ops, SparseCore 0:
  12.0 86.8 all-gather.11
Sparse Core Ops, SparseCore 1:
  121.2 27.2 all-gather.7
  150.2 28.1 all-gather.5
  180.0 26.0 all-gather.9
